TPU v7x, 256 devices: a whole 4x4x8 slice. The times are simulated.
256 devices in a mesh: seq: 64 (over z, y, core), tp: 4 (over x).
Axes of the slice: x: 4, y: 4, z: 8, core: 2. Of those that a mesh axis runs over, the one named last changes fastest.
Arguments:
- text_query_matrix: bfloat16 [16384, 8192], P('seq', 'tp'), may hold values from -12 to 12
- vision: bfloat16 [16384, 8192], P(('seq', 'tp')), may hold values from -12 to 12
- key_matrix: bfloat16 [8192, 1024], P(None, 'tp'), may hold values from -0.0625 to 0.0625
- value_matrix: bfloat16 [8192, 1024], P(None, 'tp'), may hold values from -0.0625 to 0.0625
- query_norm_gain: float32 [128], replicated, may hold values from 0.5 to 1.5
- key_gain: float32 [128], replicated, may hold values from 0.5 to 1.5
- block_mask: int32 [256, 64], P('seq'), may hold values from 0 to 1, as said below
Outputs:
- attended: bfloat16 [16384, 8192], P('seq', 'tp')
Inputs may be any that keep to these rules, and one draw needn't show every extreme that they name: block_mask[b, i] is 1 on exactly one run of consecutive blocks b; the run starts in the blocks of text shard i (blocks i * 4 to (i + 1) * 4 - 1) and ends at or before the last block of text shard i + 3; in every draw some image's run ends exactly at that last block.
All inputs are finite; a program needn't handle non-finite values.
Results may differ from a plain program's by a relative error of at most 0.0076.
Values may be sent and summed in bfloat16 or wider, within the bound.
No kernel may reach another device: no remote copies, remote signals or barrier semaphores. Data moves between devices by JAX's collectives and lax.ppermute only.
A program may use at most 128 MiB of HBM per device.

v0:
```python
import jax
import jax.numpy as jnp
from jax import lax
from jax.sharding import PartitionSpec as P

HEAD_SIZE = 128
REACH = 4
BLOCK = 64


def shifted(value, axis, by):
    length = lax.axis_size(axis)
    pairs = [(i, i + by) for i in range(length) if 0 <= i + by < length]
    return lax.ppermute(value, axis, pairs)


def heads_normalized(tensor, scale_gain):
    return (
        tensor * lax.rsqrt(jnp.mean(tensor * tensor, axis=-1, keepdims=True) + 1e-05) * scale_gain
    )


def project(vision_rows, key_matrix, value_matrix, key_gain):
    kv_heads = key_matrix.shape[1] // HEAD_SIZE
    count = vision_rows.shape[0]
    key_projected = jnp.dot(vision_rows, key_matrix, preferred_element_type=jnp.float32).reshape(
        count, kv_heads, HEAD_SIZE
    )
    key_matrix_rows = (
        heads_normalized(key_projected, key_gain)
        .astype(jnp.bfloat16)
        .reshape(count, kv_heads * HEAD_SIZE)
    )
    value_matrix_rows = jnp.dot(
        vision_rows, value_matrix, preferred_element_type=jnp.float32
    ).astype(jnp.bfloat16)
    return jnp.stack([key_matrix_rows, value_matrix_rows])


def attend(carried, kv_block, weight_col, queries):
    totals, accumulated = carried
    kv_heads = queries.shape[1]
    score_scale = HEAD_SIZE ** (-0.5)
    split_block = kv_block.reshape(2, kv_block.shape[1], kv_heads, HEAD_SIZE)
    new_totals = []
    new_sums = []
    for kv_index in range(kv_heads):
        scores = (
            jnp.einsum(
                "tgd,kd->gtk",
                queries[:, kv_index],
                split_block[0, :, kv_index],
                preferred_element_type=jnp.float32,
            )
            * score_scale
        )
        weights = jnp.exp(scores) * weight_col[None, :, None]
        new_totals.append(totals[kv_index] + jnp.sum(weights, axis=2))
        new_sums.append(
            accumulated[:, kv_index]
            + jnp.einsum(
                "gtk,kd->tgd",
                weights.astype(jnp.bfloat16),
                split_block[1, :, kv_index],
                preferred_element_type=jnp.float32,
            )
        )
    return (jnp.stack(new_totals), jnp.stack(new_sums, axis=1))


def body(
    text_query_matrix, vision, key_matrix, value_matrix, query_norm_gain, key_gain, block_mask
):
    vision_rows = lax.all_gather(vision, "tp", axis=0, tiled=True)
    kv_heads = key_matrix.shape[1] // HEAD_SIZE
    query_group_width = text_query_matrix.shape[1] // HEAD_SIZE // kv_heads
    text_rows = text_query_matrix.shape[0]
    queries = heads_normalized(
        text_query_matrix.astype(jnp.float32).reshape(
            text_rows, kv_heads, query_group_width, HEAD_SIZE
        ),
        query_norm_gain,
    ).astype(jnp.bfloat16)
    arrivals = [vision_rows] + [
        shifted(vision_rows, "seq", distance) for distance in range(1, REACH)
    ]
    kv_blocks = [project(arrived, key_matrix, value_matrix, key_gain) for arrived in arrivals]
    carried = (
        jnp.zeros((kv_heads, query_group_width, text_rows), jnp.float32),
        jnp.zeros((text_rows, kv_heads, query_group_width, HEAD_SIZE), jnp.float32),
    )
    position = lax.axis_index("seq")
    for distance in range(REACH):
        image_index = position - distance
        column = lax.dynamic_slice_in_dim(block_mask, jnp.maximum(image_index, 0), 1, 1)[:, 0]
        column = jnp.where(image_index >= 0, column, jnp.zeros_like(column))
        weight_col = jnp.repeat(column.astype(jnp.float32), BLOCK)
        carried = attend(carried, kv_blocks[distance], weight_col, queries)
    totals, accumulated = carried
    totals_t = jnp.transpose(totals, (2, 0, 1))[..., None]
    has_image = totals_t > 0
    averaged = accumulated / jnp.where(has_image, totals_t, jnp.ones_like(totals_t))
    result_rows = jnp.where(has_image, averaged, jnp.zeros_like(averaged))
    return result_rows.astype(jnp.bfloat16).reshape(
        text_rows, kv_heads * query_group_width * HEAD_SIZE
    )


def solution(mesh):
    placed = (
        P("seq", "tp"),
        P(("seq", "tp"), None),
        P(None, "tp"),
        P(None, "tp"),
        P(),
        P(),
        P("seq", None),
    )
    return jax.shard_map(
        body, mesh=mesh, in_specs=placed, out_specs=P("seq", "tp"), check_vma=False
    )
```

profile of v0, /device:TPU:32, one launch (start us, length us, event | category | flops | bytes accessed | tf_op | source)
XLA Modules:
  0.0 340.6 jit_solution(10686656299928051354)
XLA Ops:
  7.3 55.3 %all-gather.2.cloned.1.call-done = bf16[256,8192]{1,0:T(8,128)(2,1)} async-done(((bf16[64,8192]{1,0:T(8,128)(2,1)}), bf16[256,8192]{1,0:T(8,128)(2,1)}) %all-gather.2.cloned.1.call-update) | async-done | bytes 4194320 | tf_op jit(solution)/shard_map/all_gather | solution.py:74
  62.6 2.8 collective-permute-start.2
  65.4 3.4 collective-permute-start.1
  68.8 2.9 collective-permute-start
  71.8 1.1 convert_reduce_fusion
  73.5 1.5 copy.19
  76.5 1.2 copy-done
  77.7 4.0 %bitcast_reduce_fusion.11 = (f32[256,2]{0,1:T(2,128)S(1)}, f32[256,256]{0,1:T(8,128)S(1)}) fusion(bf16[256,8192]{1,0:T(8,128)(2,1)} %all-gather.2.cloned.1.call-done, bf16[8192,256]{1,0:T(8,128)(2,1)S(1)} %copy-done), kind=kOutput, calls=%fused_computation.72 | convolution fusion | flops 1073872384 | bytes 8652800 | tf_op jit(solution)/shard_map/dot_general | solution.py:26
  81.9 5.3 %convolution_convert_fusion.3 = bf16[256,256]{0,1:T(8,128)(2,1)S(1)} fusion(bf16[256,8192]{1,0:T(8,128)(2,1)} %all-gather.2.cloned.1.call-done, bf16[8192,256]{1,0:T(8,128)(2,1)} %param.10), kind=kOutput, calls=%fused_computation.40 | convolution fusion | flops 1073807360 | bytes 8519680 | tf_op jit(solution)/shard_map/dot_general | solution.py:34
  87.2 67.9 %collective-permute-done.2 = bf16[256,8192]{1,0:T(8,128)(2,1)} collective-permute-done((bf16[256,8192]{1,0:T(8,128)(2,1)}, bf16[256,8192]{1,0:T(8,128)(2,1)}, u32[]{:S(2)}, u32[]{:S(2)}) %collective-permute-start.2) | collective-permute-done | bytes 4194336 | tf_op jit(solution)/shard_map/ppermute | solution.py:14
  155.1 4.0 %bitcast_reduce_fusion.8 = (f32[256,2]{0,1:T(2,128)S(1)}, f32[256,256]{0,1:T(8,128)S(1)}) fusion(bf16[256,8192]{1,0:T(8,128)(2,1)} %collective-permute-done.2, bf16[8192,256]{1,0:T(8,128)(2,1)S(1)} %copy-done.1), kind=kOutput, calls=%fused_computation.69 | convolution fusion | flops 1073872384 | bytes 8652800 | tf_op jit(solution)/shard_map/dot_general | solution.py:26
  159.3 97.8 %collective-permute-done.1 = bf16[256,8192]{1,0:T(8,128)(2,1)} collective-permute-done((bf16[256,8192]{1,0:T(8,128)(2,1)}, bf16[256,8192]{1,0:T(8,128)(2,1)}, u32[]{:S(2)}, u32[]{:S(2)}) %collective-permute-start.1) | collective-permute-done | bytes 4194336 | tf_op jit(solution)/shard_map/ppermute | solution.py:14
  257.1 5.2 %bitcast_reduce_fusion.9 = (f32[256,2]{0,1:T(2,128)S(1)}, f32[256,256]{0,1:T(8,128)S(1)}) fusion(bf16[256,8192]{1,0:T(8,128)(2,1)} %collective-permute-done.1, bf16[8192,256]{1,0:T(8,128)(2,1)} %param.9), kind=kOutput, calls=%fused_computation.70 | convolution fusion | flops 1073872384 | bytes 8652800 | tf_op jit(solution)/shard_map/dot_general | solution.py:26
  262.5 40.5 %collective-permute-done = bf16[256,8192]{1,0:T(8,128)(2,1)} collective-permute-done((bf16[256,8192]{1,0:T(8,128)(2,1)}, bf16[256,8192]{1,0:T(8,128)(2,1)}, u32[]{:S(2)}, u32[]{:S(2)}) %collective-permute-start) | collective-permute-done | bytes 4194336 | tf_op jit(solution)/shard_map/ppermute | solution.py:14
  302.9 5.2 %bitcast_reduce_fusion.10 = (f32[256,2]{0,1:T(2,128)S(1)}, f32[256,256]{0,1:T(8,128)S(1)}) fusion(bf16[256,8192]{1,0:T(8,128)(2,1)} %collective-permute-done, bf16[8192,256]{1,0:T(8,128)(2,1)} %param.9), kind=kOutput, calls=%fused_computation.71 | convolution fusion | flops 1073872384 | bytes 8652800 | tf_op jit(solution)/shard_map/dot_general | solution.py:26
  310.4 0.9 bitcast_reduce_fusion.4
  311.3 1.1 bitcast_reduce_fusion.6
  312.4 0.9 bitcast_reduce_fusion.5
  313.4 0.9 bitcast_reduce_fusion.7
  315.4 1.1 copy-done.2
  316.5 4.0 %convolution_convert_fusion.2 = bf16[256,256]{0,1:T(8,128)(2,1)S(1)} fusion(bf16[256,8192]{1,0:T(8,128)(2,1)} %collective-permute-done, bf16[8192,256]{1,0:T(8,128)(2,1)S(1)} %copy-done.2), kind=kOutput, calls=%fused_computation.39 | convolution fusion | flops 1073807360 | bytes 8519680 | tf_op jit(solution)/shard_map/dot_general | solution.py:34
  321.1 4.0 %convolution_convert_fusion.1 = bf16[256,256]{0,1:T(8,128)(2,1)S(1)} fusion(bf16[256,8192]{1,0:T(8,128)(2,1)} %collective-permute-done.1, bf16[8192,256]{1,0:T(8,128)(2,1)S(1)} %copy-done.2), kind=kOutput, calls=%fused_computation.38 | convolution fusion | flops 1073807360 | bytes 8519680 | tf_op jit(solution)/shard_map/dot_general | solution.py:34
  325.7 4.0 %convolution_convert_fusion = bf16[256,256]{0,1:T(8,128)(2,1)S(1)} fusion(bf16[256,8192]{1,0:T(8,128)(2,1)} %collective-permute-done.2, bf16[8192,256]{1,0:T(8,128)(2,1)S(1)} %copy-done.2), kind=kOutput, calls=%fused_computation.37 | convolution fusion | flops 1073807360 | bytes 8519680 | tf_op jit(solution)/shard_map/dot_general | solution.py:34
  332.4 1.4 copy.32
  (46 shorter events, 10.2 us)
Async XLA Ops:
  6.5 56.1 %all-gather.2.cloned.1.call-start = ((), (), s32[]{:S(2)}) async-start(), calls=%async_computation | async-start | bytes 5242880 | tf_op jit(solution)/shard_map/all_gather | solution.py:74
  62.6 92.5 %collective-permute-start.2 = (bf16[256,8192]{1,0:T(8,128)(2,1)}, bf16[256,8192]{1,0:T(8,128)(2,1)}, u32[]{:S(2)}, u32[]{:S(2)}) collective-permute-start(bf16[256,8192]{1,0:T(8,128)(2,1)} %all-gather.2.cloned.1.call-done), channel_id=1, source_target_pairs={{0,12},{4,16},{8,20},{12,24},{16,28},{20,32},{24,36},{28,40},{32,4... | collective-permute-start | bytes 12582920 | tf_op jit(solution)/shard_map/ppermute | solution.py:14
  65.4 191.7 %collective-permute-start.1 = (bf16[256,8192]{1,0:T(8,128)(2,1)}, bf16[256,8192]{1,0:T(8,128)(2,1)}, u32[]{:S(2)}, u32[]{:S(2)}) collective-permute-start(bf16[256,8192]{1,0:T(8,128)(2,1)} %all-gather.2.cloned.1.call-done), channel_id=1, source_target_pairs={{0,8},{4,12},{8,16},{12,20},{16,24},{20,28},{24,32},{28,36},{32,40... | collective-permute-start | bytes 12582920 | tf_op jit(solution)/shard_map/ppermute | solution.py:14
  68.8 234.1 %collective-permute-start = (bf16[256,8192]{1,0:T(8,128)(2,1)}, bf16[256,8192]{1,0:T(8,128)(2,1)}, u32[]{:S(2)}, u32[]{:S(2)}) collective-permute-start(bf16[256,8192]{1,0:T(8,128)(2,1)} %all-gather.2.cloned.1.call-done), channel_id=1, source_target_pairs={{0,4},{4,8},{8,12},{12,16},{16,20},{20,24},{24,28},{28,32},{32,36}... | collective-permute-start | bytes 12582920 | tf_op jit(solution)/shard_map/ppermute | solution.py:14
  75.0 0.8 copy-start.4
  75.5 2.2 copy-start
  81.9 73.2 %copy-start.1 = (bf16[8192,256]{1,0:T(8,128)(2,1)S(1)}, bf16[8192,256]{1,0:T(8,128)(2,1)}, u32[]{:S(2)}) copy-start(bf16[8192,256]{1,0:T(8,128)(2,1)} %param.9) | copy-start | bytes 12582916
  262.4 45.9 %copy-start.3 = (f32[128]{0:T(128)S(1)}, f32[128]{0:T(128)}, u32[]{:S(2)}) copy-start(f32[128]{0:T(128)} %param.12) | copy-start | bytes 1540
  314.3 2.2 copy-start.2
Sparse Core Ops, SparseCore 0:
  9.2 53.3 all-gather.1
where the time goes:
time: 341 us
  waiting for transfers between devices  262 us (77%)
  matrix products  46 us (13%)
  between operations  13.7 us (4%)
  starting transfers between devices  9.15 us (3%)
  local copies, waits for them, and re-layouts  6.85 us (2%)
    ppermute x3, waiting for transfers between devices, shifted(): return lax.ppermute(value, axis, pairs)  206 us
    all_gather x1, waiting for transfers between devices, body(): vision_rows = lax.all_gather(vision, 'tp', axis=0, tiled=True)  55.3 us
    dot_general x4, matrix products, project(): jnp.dot(vision_rows, key_matrix, preferred_element_type=jnp.float32)  18.5 us
    dot_general x4, matrix products, project(): jnp.dot(vision_rows, value_matrix, preferred_element_type=jnp.float32)  17.4 us
    ppermute x3, starting transfers between devices, shifted(): return lax.ppermute(value, axis, pairs)  9.15 us
  transfers between devices with their start and end apart: 4, of which 4 were waited for; matrix products, arithmetic and copies ran while one was open for 7% of the time, Pallas kernels for 0%

commit v1 on v0

--- a/solution.py
+++ b/solution.py
@@ -71,7 +71,9 @@
 def body(
     text_query_matrix, vision, key_matrix, value_matrix, query_norm_gain, key_gain, block_mask
 ):
-    vision_rows = lax.all_gather(vision, "tp", axis=0, tiled=True)
+    vision_rows = jnp.concatenate(
+        lax.all_to_all(jnp.stack([vision] * lax.axis_size("tp")), "tp", 0, 0), axis=0
+    )
     kv_heads = key_matrix.shape[1] // HEAD_SIZE
     query_group_width = text_query_matrix.shape[1] // HEAD_SIZE // kv_heads
     text_rows = text_query_matrix.shape[0]

time: 341 us -> 326 us (0.956)
  waiting for transfers between devices: 262 us -> 198 us
  blocking collectives: 0 us -> 53.1 us
  between operations: 13.7 us -> 0.36 us
  local copies, waits for them, and re-layouts: 6.85 us -> 14.9 us
    all_gather x1 -> x0, waiting for transfers between devices: 55.3 us -> none  [body(): vision_rows = lax.all_gather(vision, 'tp', axis=0, tiled=True)]
    all_to_all x0 -> x1, blocking collectives: none -> 53.1 us  [body(): lax.all_to_all(jnp.stack([vision] * lax.axis_size('tp')), 'tp', 0, 0)]
    ppermute x3, waiting for transfers between devices: 206 us -> 198 us  [shifted(): return lax.ppermute(value, axis, pairs)]
    dot_general x0 -> x1, local copies, waits for them, and re-layouts: none -> 6.39 us  [project(): jnp.dot(vision_rows, key_matrix, preferred_element_type=jnp.float32)]
  transfers between devices with their start and end apart: 4 -> 3, of which waited for: 4 -> 3; matrix products, arithmetic and copies ran while one was open for 7% -> 10% of each run, Pallas kernels for 0% -> 0%
where the time goes in v1:
time: 326 us; the launch traced here: 325 us
  waiting for transfers between devices  198 us (61%)
  blocking collectives  53.1 us (16%)
  matrix products  45.6 us (14%)
  local copies, waits for them, and re-layouts  14.9 us (5%)
  starting transfers between devices  9.56 us (3%)
    ppermute x3, waiting for transfers between devices, shifted(): return lax.ppermute(value, axis, pairs)  198 us
    all_to_all x1, blocking collectives, body(): lax.all_to_all(jnp.stack([vision] * lax.axis_size('tp')), 'tp', 0, 0)  53.1 us
    dot_general x4, matrix products, project(): jnp.dot(vision_rows, key_matrix, preferred_element_type=jnp.float32)  19.4 us
    dot_general x4, matrix products, project(): jnp.dot(vision_rows, value_matrix, preferred_element_type=jnp.float32)  16.1 us
    ppermute x3, starting transfers between devices, shifted(): return lax.ppermute(value, axis, pairs)  9.56 us
  transfers between devices with their start and end apart: 3, of which 3 were waited for; matrix products, arithmetic and copies ran while one was open for 10% of the time, Pallas kernels for 0%

profile of v1, /device:TPU:32, one launch (start us, length us, event | category | flops | bytes accessed | tf_op | source)
XLA Modules:
  0.0 324.5 jit_solution(2544374052489643171)
XLA Ops:
  0.0 1.7 stack.39
  1.7 53.1 %all_to_all.5 = bf16[4,64,8192]{2,1,0:T(8,128)(2,1)} all-to-all(bf16[4,64,8192]{2,1,0:T(8,128)(2,1)S(1)} %stack.39), channel_id=1, replica_groups=mesh['seq'=64,'tp'=4] {'tp'}, dimensions={0} | all-to-all | bytes 8388608 | tf_op jit(solution)/shard_map/all_to_all | solution.py:75
  54.8 2.0 collective-permute-start.2
  56.9 3.5 %collective-permute-start.1 = (bf16[256,8192]{1,0:T(8,128)(2,1)}, bf16[256,8192]{1,0:T(8,128)(2,1)}, u32[]{:S(2)}, u32[]{:S(2)}) collective-permute-start(bf16[256,8192]{1,0:T(8,128)(2,1)} %bitcast), channel_id=1, source_target_pairs={{0,8},{4,12},{8,16},{12,20},{16,24},{20,28},{24,32},{28,36},{32,40... | collective-permute-start | bytes 12582920 | tf_op jit(solution)/shard_map/ppermute | solution.py:14
  61.2 4.0 %collective-permute-start = (bf16[256,8192]{1,0:T(8,128)(2,1)}, bf16[256,8192]{1,0:T(8,128)(2,1)}, u32[]{:S(2)}, u32[]{:S(2)}) collective-permute-start(bf16[256,8192]{1,0:T(8,128)(2,1)} %bitcast), channel_id=1, source_target_pairs={{0,4},{4,8},{8,12},{12,16},{16,20},{20,24},{24,28},{28,32},{32,36}... | collective-permute-start | bytes 12582920 | tf_op jit(solution)/shard_map/ppermute | solution.py:14
  66.6 6.4 %copy.48 = bf16[256,8192]{1,0:T(8,128)(2,1)} copy(bf16[256,8192]{0,1:T(8,128)(2,1)} %bitcast.200) | data formatting | bytes 8388608 | tf_op jit(solution)/shard_map/dot_general | solution.py:26
  73.8 4.9 %multiply_reduce_fusion.1 = (f32[256,2]{0,1:T(2,128)S(1)}, f32[256,2,128]{0,2,1:T(8,128)S(1)}) fusion(bf16[256,8192,1]{1,0,2:T(8,128)(2,1)} %bitcast.1, bf16[2,128,8192]{2,1,0:T(8,128)(2,1)} %bitcast.202), kind=kOutput, calls=%fused_computation.76 | convolution fusion | flops 1073872384 | bytes 8652800 | tf_op jit(solution)/shard_map/dot_general | solution.py:26
  79.2 4.0 %convolution_convert_fusion.3 = bf16[256,256]{0,1:T(8,128)(2,1)S(1)} fusion(bf16[256,8192]{1,0:T(8,128)(2,1)} %bitcast, bf16[8192,256]{1,0:T(8,128)(2,1)S(1)} %copy-done.1), kind=kOutput, calls=%fused_computation.40 | convolution fusion | flops 1073807360 | bytes 8519680 | tf_op jit(solution)/shard_map/dot_general | solution.py:34
  83.8 0.9 bitcast_reduce_fusion.7
  85.3 60.2 %collective-permute-done.2 = bf16[256,8192]{1,0:T(8,128)(2,1)} collective-permute-done((bf16[256,8192]{1,0:T(8,128)(2,1)}, bf16[256,8192]{1,0:T(8,128)(2,1)}, u32[]{:S(2)}, u32[]{:S(2)}) %collective-permute-start.2) | collective-permute-done | bytes 4194336 | tf_op jit(solution)/shard_map/ppermute | solution.py:14
  145.5 4.0 %bitcast_reduce_fusion.8 = (f32[256,2]{0,1:T(2,128)S(1)}, f32[256,256]{0,1:T(8,128)S(1)}) fusion(bf16[256,8192]{1,0:T(8,128)(2,1)} %collective-permute-done.2, bf16[8192,256]{1,0:T(8,128)(2,1)S(1)} %copy-done), kind=kOutput, calls=%fused_computation.69 | convolution fusion | flops 1073872384 | bytes 8652800 | tf_op jit(solution)/shard_map/dot_general | solution.py:26
  150.4 96.9 %collective-permute-done.1 = bf16[256,8192]{1,0:T(8,128)(2,1)} collective-permute-done((bf16[256,8192]{1,0:T(8,128)(2,1)}, bf16[256,8192]{1,0:T(8,128)(2,1)}, u32[]{:S(2)}, u32[]{:S(2)}) %collective-permute-start.1) | collective-permute-done | bytes 4194336 | tf_op jit(solution)/shard_map/ppermute | solution.py:14
  247.3 5.2 %bitcast_reduce_fusion.9 = (f32[256,2]{0,1:T(2,128)S(1)}, f32[256,256]{0,1:T(8,128)S(1)}) fusion(bf16[256,8192]{1,0:T(8,128)(2,1)} %collective-permute-done.1, bf16[8192,256]{1,0:T(8,128)(2,1)} %param.9), kind=kOutput, calls=%fused_computation.70 | convolution fusion | flops 1073872384 | bytes 8652800 | tf_op jit(solution)/shard_map/dot_general | solution.py:26
  253.3 41.0 %collective-permute-done = bf16[256,8192]{1,0:T(8,128)(2,1)} collective-permute-done((bf16[256,8192]{1,0:T(8,128)(2,1)}, bf16[256,8192]{1,0:T(8,128)(2,1)}, u32[]{:S(2)}, u32[]{:S(2)}) %collective-permute-start) | collective-permute-done | bytes 4194336 | tf_op jit(solution)/shard_map/ppermute | solution.py:14
  294.3 5.2 %bitcast_reduce_fusion.10 = (f32[256,2]{0,1:T(2,128)S(1)}, f32[256,256]{0,1:T(8,128)S(1)}) fusion(bf16[256,8192]{1,0:T(8,128)(2,1)} %collective-permute-done, bf16[8192,256]{1,0:T(8,128)(2,1)} %param.9), kind=kOutput, calls=%fused_computation.71 | convolution fusion | flops 1073872384 | bytes 8652800 | tf_op jit(solution)/shard_map/dot_general | solution.py:26
  300.4 1.4 multiply_convert_fusion.1
  303.1 1.1 bitcast_reduce_fusion.4
  304.2 0.9 bitcast_reduce_fusion.5
  305.1 0.9 bitcast_reduce_fusion.6
  306.1 1.2 copy-done.2
  307.3 4.0 %convolution_convert_fusion.2 = bf16[256,256]{0,1:T(8,128)(2,1)S(1)} fusion(bf16[256,8192]{1,0:T(8,128)(2,1)} %collective-permute-done, bf16[8192,256]{1,0:T(8,128)(2,1)S(1)} %copy-done.2), kind=kOutput, calls=%fused_computation.39 | convolution fusion | flops 1073807360 | bytes 8519680 | tf_op jit(solution)/shard_map/dot_general | solution.py:34
  311.9 4.0 %convolution_convert_fusion.1 = bf16[256,256]{0,1:T(8,128)(2,1)S(1)} fusion(bf16[256,8192]{1,0:T(8,128)(2,1)} %collective-permute-done.1, bf16[8192,256]{1,0:T(8,128)(2,1)S(1)} %copy-done.2), kind=kOutput, calls=%fused_computation.38 | convolution fusion | flops 1073807360 | bytes 8519680 | tf_op jit(solution)/shard_map/dot_general | solution.py:34
  316.5 4.0 %convolution_convert_fusion = bf16[256,256]{0,1:T(8,128)(2,1)S(1)} fusion(bf16[256,8192]{1,0:T(8,128)(2,1)} %collective-permute-done.2, bf16[8192,256]{1,0:T(8,128)(2,1)S(1)} %copy-done.2), kind=kOutput, calls=%fused_computation.37 | convolution fusion | flops 1073807360 | bytes 8519680 | tf_op jit(solution)/shard_map/dot_general | solution.py:34
  323.1 1.4 copy.37
  (51 shorter events, 12.0 us)
Async XLA Ops:
  1.7 58.7 %copy-start.3 = (bf16[256,2048]{1,0:T(8,128)(2,1)S(1)}, bf16[256,2048]{1,0:T(8,128)(2,1)}, u32[]{:S(2)}) copy-start(bf16[256,2048]{1,0:T(8,128)(2,1)} %param.7) | copy-start | bytes 3145732
  54.8 10.4 %copy-start.4 = (s32[4,64]{1,0:T(4,128)S(1)}, s32[4,64]{1,0:T(4,128)}, u32[]{:S(2)}) copy-start(s32[4,64]{1,0:T(4,128)} %param.13) | copy-start | bytes 3076
  54.8 90.6 %collective-permute-start.2 = (bf16[256,8192]{1,0:T(8,128)(2,1)}, bf16[256,8192]{1,0:T(8,128)(2,1)}, u32[]{:S(2)}, u32[]{:S(2)}) collective-permute-start(bf16[256,8192]{1,0:T(8,128)(2,1)} %bitcast), channel_id=1, source_target_pairs={{0,12},{4,16},{8,20},{12,24},{16,28},{20,32},{24,36},{28,40},{32,4... | collective-permute-start | bytes 12582920 | tf_op jit(solution)/shard_map/ppermute | solution.py:14
  56.9 190.4 %collective-permute-start.1 = (bf16[256,8192]{1,0:T(8,128)(2,1)}, bf16[256,8192]{1,0:T(8,128)(2,1)}, u32[]{:S(2)}, u32[]{:S(2)}) collective-permute-start(bf16[256,8192]{1,0:T(8,128)(2,1)} %bitcast), channel_id=1, source_target_pairs={{0,8},{4,12},{8,16},{12,20},{16,24},{20,28},{24,32},{28,36},{32,40... | collective-permute-start | bytes 12582920 | tf_op jit(solution)/shard_map/ppermute | solution.py:14
  61.2 233.1 %collective-permute-start = (bf16[256,8192]{1,0:T(8,128)(2,1)}, bf16[256,8192]{1,0:T(8,128)(2,1)}, u32[]{:S(2)}, u32[]{:S(2)}) collective-permute-start(bf16[256,8192]{1,0:T(8,128)(2,1)} %bitcast), channel_id=1, source_target_pairs={{0,4},{4,8},{8,12},{12,16},{16,20},{20,24},{24,28},{28,32},{32,36}... | collective-permute-start | bytes 12582920 | tf_op jit(solution)/shard_map/ppermute | solution.py:14
  66.6 6.4 %copy-start.6 = (f32[128]{0:T(128)S(1)}, f32[128]{0:T(128)}, u32[]{:S(2)}) copy-start(f32[128]{0:T(128)} %param.11) | copy-start | bytes 1540
  73.7 4.9 %copy-start.5 = (f32[128]{0:T(128)S(1)}, f32[128]{0:T(128)}, u32[]{:S(2)}) copy-start(f32[128]{0:T(128)} %param.12) | copy-start | bytes 1540
  73.7 5.5 %copy-start.1 = (bf16[8192,256]{1,0:T(8,128)(2,1)S(1)}, bf16[8192,256]{1,0:T(8,128)(2,1)}, u32[]{:S(2)}) copy-start(bf16[8192,256]{1,0:T(8,128)(2,1)} %param.10) | copy-start | bytes 12582916
  83.8 61.7 %copy-start = (bf16[8192,256]{1,0:T(8,128)(2,1)S(1)}, bf16[8192,256]{1,0:T(8,128)(2,1)}, u32[]{:S(2)}) copy-start(bf16[8192,256]{1,0:T(8,128)(2,1)} %param.9) | copy-start | bytes 12582916
  305.1 2.2 copy-start.2
